TPU v7x, 128 devices: a whole 4x4x4 slice. The times are simulated.
128 devices in a mesh: scene: 128 (over x, z, y, core).
Axes of the slice: x: 4, y: 4, z: 4, core: 2. Of those that a mesh axis runs over, the one named last changes fastest.
Arguments:
- first_scene: int32 [3072], P('scene'), may hold values from 0 to 1023, as said below
- second_scene: int32 [3072], P('scene'), may hold values from 0 to 1023, as said below
- rad_first: bfloat16 [3072, 224, 128], P('scene'), may hold values from 0.5 to 1.5
- rad_second: bfloat16 [3072, 224, 128], P('scene'), may hold values from 0.5 to 1.5
- pos_first: int32 [3072, 128], P('scene'), may hold values from 0 to 1023
- pos_second: int32 [3072, 128], P('scene'), may hold values from 0 to 1023
- prior_weight: float32 [1024], P('scene'), may hold values from 1 to 10
Outputs:
- solution: float32 [1024, 28672], P('scene')
- residual: float32 [1024, 28672], P('scene')
Inputs may be any that keep to these rules, and one draw needn't show every extreme that they name: first_scene of every pair lies among the 8 scenes of the device that holds the pair, in strip order. second_scene equals (first_scene + k) modulo 1024 for some k from 1 to 8; the strip closes on itself, and k = 8 occurs on every device.
All inputs are finite; a program needn't handle non-finite values.
Results may differ from a plain program's by a relative error of at most 0.0003.
Values sent between devices are 32-bit elements; how exact they have to be, the bound alone decides.
A program may use at most 128 MiB of HBM per device.

v0:
```python
import functools
import math

import jax
import jax.numpy as jnp
from jax import lax
from jax.experimental import pallas as pl
from jax.experimental.pallas import tpu as pltpu
from jax.sharding import PartitionSpec as P

TERMS = 64
COLS = 1024
LANES = 128
OWNED = 8
UNROLL = 4
MESH = pl.DeviceIdType.MESH
F32 = jnp.float32
BF16 = jnp.bfloat16


def row_chunks(bands):
    return ((0, bands // 2), (bands // 2, bands // 2))


def groups_of(n):
    return ((8, 1), (4, 8), (4, 32)) if n == 128 else ((n, 1),)


def split(x):
    hi = x.astype(BF16)
    lo = (x - hi.astype(F32)).astype(BF16)
    return hi, lo


def halves(x):
    hi, lo = split(x)
    return jnp.concatenate([hi, lo], axis=1)


def low_lanes(rows):
    return lax.broadcasted_iota(jnp.int32, (rows, LANES), 1) < TERMS


def swap(x):
    return pltpu.roll(x, TERMS, 1)


def fold(x):
    return jnp.sum(x.reshape(x.shape[0] // 8, 8, LANES), axis=0)


def kernel(
    n,
    fs_ref, ss_ref, pw_ref, ra_ref, rb_ref, qa_ref, qb_ref,
    out_s, out_r,
    leg_a, leg_b, wj_a, wj_b, wt, w2_a, w2_b,
    run, run_d, run_o, coef,
    own0, ahead0, recv_l0, recv_r0,
    own1, ahead1, recv_l1, recv_r1,
    own2, ahead2, recv_l2,
    tile_l, tile_r, recv_tl, recv_tr,
    res, zz, inv, az, ww, diag_o, prior, macc,
    red_src, red_dst,
    slot, prev, last,
    sem_s0, sem_r0, sem_s1, sem_r1, sem_s2, sem_r2, sem_t, red_ssem, red_rsem,
):
    me = lax.axis_index("scene")
    right, left = lax.rem(me + 1, n), lax.rem(me + n - 1, n)
    pairs, bands = ra_ref.shape[0], ra_ref.shape[1]
    halfs = 2 * pairs
    chunks = row_chunks(bands)
    groups = groups_of(n)
    peers = []
    for size, stride in groups:
        place = (me // stride) % size
        for j in range(1, size):
            peers.append((me - place * stride) + ((place + j) % size) * stride)

    barrier = pltpu.get_barrier_semaphore()
    for other in [left, right] + peers:
        pl.semaphore_signal(barrier, inc=1, device_id=(other,), device_id_type=MESH)

    for i in range(2 * OWNED):
        last[i] = halfs

    def link(p, carry):
        a = fs_ref[p] - me * OWNED
        b = ss_ref[p] - me * OWNED
        b = jnp.where(b < 0, b + n * OWNED, b)
        for h, scene in ((2 * p, a), (2 * p + 1, b)):
            scene = jnp.clip(scene, 0, 2 * OWNED - 1)
            slot[h] = scene
            before = jnp.int32(halfs)
            after = []
            for i in range(2 * OWNED):
                hit = scene == i
                before = jnp.where(hit, carry[i], before)
                after.append(jnp.where(hit, h, carry[i]))
            prev[h] = before
            carry = tuple(after)
        return carry

    ends = lax.fori_loop(0, pairs, link, tuple(jnp.int32(halfs) for _ in range(2 * OWNED)))
    for i in range(2 * OWNED):
        last[i] = ends[i]

    for q_ref, leg in ((qa_ref, leg_a), (qb_ref, leg_b)):
        sign = 1.0 if leg is leg_a else -1.0
        t = q_ref[...].astype(F32) * (2.0 / (COLS - 1)) - 1.0
        before, now = jnp.ones_like(t), t
        for k in range(TERMS):
            leg[pl.ds(k * pairs, pairs), :] = before * (sign * 0.0625 * math.sqrt(2 * k + 1))
            before, now = now, ((2 * k + 3) / (k + 2)) * t * now - ((k + 1) / (k + 2)) * before

    run[halfs] = jnp.zeros(run.shape[1:], F32)
    run_d[halfs] = jnp.zeros(run_d.shape[1:], F32)
    run_o[halfs] = jnp.zeros(run_o.shape[1:], F32)
    macc[...] = jnp.zeros(macc.shape, F32)

    def weights(p, _):
        tops = []
        for side, (leg, wj, w2) in enumerate(((leg_a, wj_a, w2_a), (leg_b, wj_b, w2_b))):
            phi = leg[pl.ds(p, TERMS, stride=pairs), :]
            hi, lo = split(phi)
            wj[p] = jnp.concatenate([hi, lo, hi, lo], axis=0)
            top = jnp.concatenate([hi.astype(F32), lo.astype(F32)], axis=0)
            tops.append(top.T.astype(BF16))
            square = phi * phi
            hi, lo = split(square)
            top = jnp.concatenate([hi.astype(F32), lo.astype(F32)], axis=0)
            turned = top.T.astype(BF16)
            w2[p] = turned
            sums = jnp.dot(jnp.ones((16, LANES), BF16), turned, preferred_element_type=F32)
            h = 2 * p + side
            run_o[h] = sums[:8] + run_o[prev[h]]
        wt[p] = jnp.concatenate(tops, axis=1)
        return 0

    lax.fori_loop(0, pairs, weights, 0)

    for s in range(2 * OWNED):
        total = run_o[last[s]]
        total = total + swap(total)
        tile = tile_l if s < OWNED else tile_r
        row = s % OWNED
        tile[pl.ds(row, 1), :] = total[:1]
    for s in range(OWNED):
        tile_l[pl.ds(OWNED + s, 1), :] = jnp.full((1, LANES), pw_ref[s], F32)

    pl.semaphore_wait(barrier, 2 + len(peers))
    tiles = [
        pltpu.make_async_remote_copy(tile_r, recv_tl, sem_t.at[0], sem_t.at[1], device_id=(right,), device_id_type=MESH),
        pltpu.make_async_remote_copy(tile_l, recv_tr, sem_t.at[2], sem_t.at[3], device_id=(left,), device_id_type=MESH),
    ]
    for copy in tiles:
        copy.start()

    def transfers(c, rows, to_right, to_left, send, recv):
        r0, size = rows
        moves = []
        for way, (pair, other) in enumerate(((to_right, right), (to_left, left))):
            if pair is not None:
                src, dst = pair
                moves.append(
                    pltpu.make_async_remote_copy(
                        src.at[:, pl.ds(r0, size), :],
                        dst.at[:, pl.ds(r0, size), :],
                        send.at[2 * c + way],
                        recv.at[2 * c + way],
                        device_id=(other,),
                        device_id_type=MESH,
                    )
                )
        return moves

    def pull(p, size, e, la, lb):
        weight = wt[p]
        weight = jnp.concatenate([weight, weight], axis=0)
        both = jnp.dot(halves(e), weight, preferred_element_type=F32)
        gain_a = jnp.dot(halves(la * e), weight[:, :LANES], preferred_element_type=F32)
        gain_b = jnp.dot(halves(lb * e), weight[:, LANES:], preferred_element_type=F32)
        low = low_lanes(size)
        for side, gain in ((0, gain_a), (1, gain_b)):
            offset = both[:, side * LANES : (side + 1) * LANES]
            term = jnp.where(low, gain, offset) + swap(jnp.where(low, offset, gain))
            h = 2 * p + side
            run[h, :size, :] = term + run[prev[h], :size, :]

    def over_pairs(body, init):
        def step(g, carry):
            for u in range(UNROLL):
                carry = body(g * UNROLL + u, carry)
            return carry

        return lax.fori_loop(0, pairs // UNROLL, step, init)

    moves0 = []
    for c, (r0, size) in enumerate(chunks):
        rows = pl.ds(r0, size)

        def start_pair(p, carry):
            la = ra_ref[p, rows, :].astype(F32)
            lb = rb_ref[p, rows, :].astype(F32)
            pull(p, size, lb - la, la, lb)
            for side, (rad, w2) in enumerate(((la, w2_a), (lb, w2_b))):
                weight = w2[p]
                weight = jnp.concatenate([weight, weight], axis=0)
                h = 2 * p + side
                term = jnp.dot(halves(rad * rad), weight, preferred_element_type=F32)
                run_d[h, :size, :] = term + run_d[prev[h], :size, :]
            return carry

        over_pairs(start_pair, 0)
        low = low_lanes(size)
        for base, buf in ((0, own0), (OWNED, ahead0)):
            for s in range(OWNED):
                buf[s, rows, :] = run[last[base + s], :size, :]
            for s in range(OWNED // 2):
                one = run_d[last[base + s], :size, :]
                two = run_d[last[base + s + OWNED // 2], :size, :]
                buf[OWNED + s, rows, :] = jnp.where(low, one, two) + swap(jnp.where(low, two, one))
        moves = transfers(c, (r0, size), (ahead0, recv_l0), (own0, recv_r0), sem_s0, sem_r0)
        for copy in moves:
            copy.start()
        moves0.append(moves)

    def spread(s, size, z):
        low = low_lanes(size)
        turned = swap(z)
        coef[s, 0, :size, :] = halves(jnp.where(low, z, turned))
        coef[s, 1, :size, :] = halves(jnp.where(low, turned, z))

    def apply_pair(rows, size, index):
        def body(p, total):
            la = ra_ref[p, rows, :].astype(F32)
            lb = rb_ref[p, rows, :].astype(F32)
            fields = []
            for side, wj in ((0, wj_a), (1, wj_b)):
                both = coef[slot[2 * p + side]]
                weight = wj[p]
                for part in range(2):
                    fields.append(jnp.dot(both[part, :size, :], weight, preferred_element_type=F32))
            e = (la * fields[0] + fields[1]) + (lb * fields[2] + fields[3])
            pull(p, size, e, la, lb)
            return total + fold(e * e)

        macc[index] += over_pairs(body, jnp.zeros((8, LANES), F32))

    for copy in tiles:
        copy.wait()
    diag_o[pl.ds(0, OWNED), :] = tile_l[pl.ds(0, OWNED), :] + recv_tl[...]
    diag_o[pl.ds(OWNED, OWNED), :] = tile_r[...] + recv_tr[pl.ds(0, OWNED), :]
    prior[pl.ds(0, OWNED), :] = tile_l[pl.ds(OWNED, OWNED), :]
    prior[pl.ds(OWNED, OWNED), :] = recv_tr[pl.ds(OWNED, OWNED), :]

    moves1 = []
    for c, (r0, size) in enumerate(chunks):
        rows = pl.ds(r0, size)
        for copy in moves0[c]:
            copy.wait()
        low = low_lanes(size)
        for base, mine, theirs in ((0, own0, recv_l0), (OWNED, ahead0, recv_r0)):
            for half in range(2):
                for i in range(OWNED // 2):
                    row = half * (OWNED // 2) + i
                    s = base + row
                    gain = mine[OWNED + i, rows, :] + theirs[OWNED + i, rows, :]
                    if half:
                        gain = swap(gain)
                    weight = prior[pl.ds(s, 1), :]
                    jacobi = jnp.where(low, gain, diag_o[pl.ds(s, 1), :]) + weight
                    inverse = 1.0 / jacobi
                    r = mine[row, rows, :] + theirs[row, rows, :]
                    z = r * inverse
                    inv[s, rows, :] = inverse
                    zz[s, rows, :] = z
                    if base == 0:
                        res[s, rows, :] = r
                        macc[0] += fold(r * z)
                        macc[1] += fold(weight * (z * z))
                    spread(s, size, z)
        apply_pair(rows, size, 1)
        for base, buf in ((0, own1), (OWNED, ahead1)):
            for s in range(OWNED):
                buf[s, rows, :] = run[last[base + s], :size, :]
        moves = transfers(c, (r0, size), (ahead1, recv_l1), (own1, recv_r1), sem_s1, sem_r1)
        for copy in moves:
            copy.start()
        moves1.append(moves)

    moves2 = []
    for c, (r0, size) in enumerate(chunks):
        rows = pl.ds(r0, size)
        for copy in moves1[c]:
            copy.wait()
        for base, mine, theirs in ((0, own1, recv_l1), (OWNED, ahead1, recv_r1)):
            for row in range(OWNED):
                s = base + row
                weight = prior[pl.ds(s, 1), :]
                image = mine[row, rows, :] + theirs[row, rows, :] + weight * zz[s, rows, :]
                w = image * inv[s, rows, :]
                if base == 0:
                    az[s, rows, :] = image
                    ww[s, rows, :] = w
                    macc[2] += fold(image * w)
                    macc[3] += fold(weight * (w * w))
                spread(s, size, w)
        apply_pair(rows, size, 3)
        for base, buf in ((0, own2), (OWNED, ahead2)):
            for s in range(OWNED):
                buf[s, rows, :] = run[last[base + s], :size, :]
        moves = transfers(c, (r0, size), (ahead2, recv_l2), None, sem_s2, sem_r2)
        for copy in moves:
            copy.start()
        moves2.append(moves)

    sums = [jnp.sum(macc[i], axis=0, keepdims=True) for i in range(4)]
    tile = jnp.concatenate(sums + [jnp.zeros((4, LANES), F32)], axis=0)
    count = 0
    for g, (size, stride) in enumerate(groups):
        red_src[g] = tile
        copies = []
        for j in range(1, size):
            copies.append(
                pltpu.make_async_remote_copy(
                    red_src.at[g], red_dst.at[count], red_ssem.at[count], red_rsem.at[count],
                    device_id=(peers[count],), device_id_type=MESH,
                )
            )
            copies[-1].start()
            count += 1
        for j, copy in enumerate(copies):
            copy.wait()
            tile = tile + red_dst[count - len(copies) + j]
    tile = jnp.sum(tile, axis=1, keepdims=True)
    m0, m1, m2, m3 = (tile[i : i + 1, :] for i in range(4))
    first = m0 / m1
    ratio = first * m2 / m1
    again = (ratio - 1.0) * m0
    second = again / (ratio * (ratio * m1 - 2.0 * first * m2) + first * first * m3)
    of_z = first + second * ratio
    of_w = -second * first

    for c, (r0, size) in enumerate(chunks):
        for copy in moves2[c]:
            copy.wait()
        half = size // 2
        low = low_lanes(half)
        for s in range(OWNED):
            weight = prior[pl.ds(s, 1), :]
            parts = []
            for odd in range(2):
                rows = pl.ds(r0 + odd, half, stride=2)
                w = ww[s, rows, :]
                last_image = own2[s, rows, :] + recv_l2[s, rows, :] + weight * w
                parts.append(
                    (
                        of_z * zz[s, rows, :] + of_w * w,
                        res[s, rows, :] - of_z * az[s, rows, :] - of_w * last_image,
                    )
                )
            for out, even, odd in ((out_s, parts[0][0], parts[1][0]), (out_r, parts[0][1], parts[1][1])):
                out[pl.ds((r0 // 2) * OWNED + s, half, stride=OWNED), :] = jnp.where(low, even, swap(odd))
                out[pl.ds((bands // 2 + r0 // 2) * OWNED + s, half, stride=OWNED), :] = jnp.where(low, swap(even), odd)


def shards(n, first_scene, second_scene, rad_first, rad_second, pos_first, pos_second, prior_weight):
    pairs, bands = rad_first.shape[:2]
    halfs = 2 * pairs
    chunks = row_chunks(bands)
    most = max(size for _, size in chunks)
    peers = sum(size - 1 for size, _ in groups_of(n))
    smem = pl.BlockSpec(memory_space=pltpu.SMEM)
    vmem = pl.BlockSpec(memory_space=pltpu.VMEM)

    def block(rows):
        return pltpu.VMEM((rows, bands, LANES), F32)

    flat = jax.ShapeDtypeStruct((bands * OWNED, LANES), F32)
    outs = pl.pallas_call(
        functools.partial(kernel, n),
        out_shape=(flat, flat),
        in_specs=[smem, smem, smem, vmem, vmem, vmem, vmem],
        out_specs=(vmem, vmem),
        scratch_shapes=[
            pltpu.VMEM((TERMS * pairs, LANES), F32),
            pltpu.VMEM((TERMS * pairs, LANES), F32),
            pltpu.VMEM((pairs, 4 * TERMS, LANES), BF16),
            pltpu.VMEM((pairs, 4 * TERMS, LANES), BF16),
            pltpu.VMEM((pairs, LANES, 2 * LANES), BF16),
            pltpu.VMEM((pairs, LANES, LANES), BF16),
            pltpu.VMEM((pairs, LANES, LANES), BF16),
            pltpu.VMEM((halfs + 1, most, LANES), F32),
            pltpu.VMEM((halfs + 1, most, LANES), F32),
            pltpu.VMEM((halfs + 1, 8, LANES), F32),
            pltpu.VMEM((2 * OWNED, 2, most, 2 * LANES), BF16),
            block(12), block(12), block(12), block(12),
            block(8), block(8), block(8), block(8),
            block(8), block(8), block(8),
            pltpu.VMEM((2 * OWNED, LANES), F32),
            pltpu.VMEM((OWNED, LANES), F32),
            pltpu.VMEM((OWNED, LANES), F32),
            pltpu.VMEM((2 * OWNED, LANES), F32),
            block(8), block(16), block(16), block(8), block(8),
            pltpu.VMEM((2 * OWNED, LANES), F32),
            pltpu.VMEM((2 * OWNED, LANES), F32),
            pltpu.VMEM((4, 8, LANES), F32),
            pltpu.VMEM((len(groups_of(n)), 8, LANES), F32),
            pltpu.VMEM((peers, 8, LANES), F32),
            pltpu.SMEM((halfs,), jnp.int32),
            pltpu.SMEM((halfs,), jnp.int32),
            pltpu.SMEM((2 * OWNED,), jnp.int32),
            pltpu.SemaphoreType.DMA((2 * len(chunks),)),
            pltpu.SemaphoreType.DMA((2 * len(chunks),)),
            pltpu.SemaphoreType.DMA((2 * len(chunks),)),
            pltpu.SemaphoreType.DMA((2 * len(chunks),)),
            pltpu.SemaphoreType.DMA((2 * len(chunks),)),
            pltpu.SemaphoreType.DMA((2 * len(chunks),)),
            pltpu.SemaphoreType.DMA((4,)),
            pltpu.SemaphoreType.DMA((peers,)),
            pltpu.SemaphoreType.DMA((peers,)),
        ],
        compiler_params=pltpu.CompilerParams(
            collective_id=0, has_side_effects=True, vmem_limit_bytes=56 * 1024 * 1024
        ),
    )(first_scene, second_scene, prior_weight, rad_first, rad_second, pos_first, pos_second)
    return tuple(
        x.reshape(bands, OWNED, LANES).transpose(1, 0, 2).reshape(OWNED, bands * LANES) for x in outs
    )


def solution(mesh):
    return jax.shard_map(
        functools.partial(shards, mesh.shape["scene"]),
        mesh=mesh,
        in_specs=(
            P("scene"),
            P("scene"),
            P("scene", None, None),
            P("scene", None, None),
            P("scene", None),
            P("scene", None),
            P("scene"),
        ),
        out_specs=(P("scene", None), P("scene", None)),
        check_vma=False,
    )
```

profile of v0, /device:TPU:1, one launch (start us, length us, event | category | flops | bytes accessed | tf_op | source)
XLA Modules:
  0.0 80.0 jit_solution(18406177428448493400)
XLA Ops:
  0.6 76.2 %shard_map.86 = (f32[1792,128]{1,0:T(8,128)}, f32[1792,128]{1,0:T(8,128)}) custom-call(s32[24]{0:T(128)} %fs_ref.1, s32[24]{0:T(128)} %ss_ref.1, f32[8]{0:T(128)} %pw_ref.1, bf16[24,224,128]{2,1,0:T(8,128)(2,1)} %ra_ref.1, bf16[24,224,128]{2,1,0:T(8,128)(2,1)} %rb_ref.1, s32[24,128]{1,0:T(8,128)} %qa_ref.1, s32[24,128]{1,0:T(8,128)} %qb_ref.1), custom_call_target="tpu_custom_call" | custom-call | tf_op jit(solution)/shard_map/pallas_call | solution.py:380
  76.9 0.0 copy-start
  76.9 2.2 %copy.11 = f32[8,28672]{1,0:T(8,128)} copy(f32[8,28672]{1,0:T(8,128)} %bitcast.11) | data formatting | bytes 1835008
  79.1 0.0 copy-done
  79.1 0.9 %copy.12 = f32[8,28672]{1,0:T(8,128)} copy(f32[8,28672]{1,0:T(8,128)S(1)} %bitcast.10) | data formatting | bytes 1835008
Async XLA Ops:
  76.9 2.3 %copy-start = (f32[1792,128]{1,0:T(8,128)S(1)}, f32[1792,128]{1,0:T(8,128)}, u32[]{:S(2)}) copy-start(f32[1792,128]{1,0:T(8,128)} %get-tuple-element.5) | copy-start | bytes 2752516
where the time goes:
time: 80.7 us; the launch traced here: 80 us
  Pallas kernels  76.2 us (94%)
  local copies, waits for them, and re-layouts  3.17 us (4%)
    pallas_call x1, Pallas kernels, shards(): pl.pallas_call(functools.partial(kernel, n), out_shape=(flat, flat), in_s...  76.2 us
    unnamed x4, local copies, waits for them, and re-layouts  3.17 us

commit v1 on v0

--- a/solution.py
+++ b/solution.py
@@ -12,14 +12,20 @@
 COLS = 1024
 LANES = 128
 OWNED = 8
-UNROLL = 4
+UNROLL = 8
+PREPARE = 4
 MESH = pl.DeviceIdType.MESH
 F32 = jnp.float32
 BF16 = jnp.bfloat16
 
 
 def row_chunks(bands):
-    return ((0, bands // 2), (bands // 2, bands // 2))
+    sizes = (64, 80, 80) if bands == 224 else (bands // 2, bands - bands // 2)
+    chunks, start = [], 0
+    for size in sizes:
+        chunks.append((start, size))
+        start += size
+    return chunks
 
 
 def groups_of(n):
@@ -51,9 +57,9 @@
 
 def kernel(
     n,
-    fs_ref, ss_ref, pw_ref, ra_ref, rb_ref, qa_ref, qb_ref,
+    fs_ref, ss_ref, pw_ref, ra_hbm, rb_hbm, qa_ref, qb_ref,
     out_s, out_r,
-    leg_a, leg_b, wj_a, wj_b, wt, w2_a, w2_b,
+    ra_ref, rb_ref, leg_a, leg_b, wj, wt, w2,
     run, run_d, run_o, coef,
     own0, ahead0, recv_l0, recv_r0,
     own1, ahead1, recv_l1, recv_r1,
@@ -62,7 +68,7 @@
     res, zz, inv, az, ww, diag_o, prior, macc,
     red_src, red_dst,
     slot, prev, last,
-    sem_s0, sem_r0, sem_s1, sem_r1, sem_s2, sem_r2, sem_t, red_ssem, red_rsem,
+    sem_s0, sem_r0, sem_s1, sem_r1, sem_s2, sem_r2, sem_t, sem_in, red_ssem, red_rsem,
 ):
     me = lax.axis_index("scene")
     right, left = lax.rem(me + 1, n), lax.rem(me + n - 1, n)
@@ -76,14 +82,31 @@
         for j in range(1, size):
             peers.append((me - place * stride) + ((place + j) % size) * stride)
 
+    loads = [
+        pltpu.make_async_copy(ra_hbm, ra_ref, sem_in.at[0]),
+        pltpu.make_async_copy(rb_hbm, rb_ref, sem_in.at[1]),
+    ]
+    for load in loads:
+        load.start()
+
     barrier = pltpu.get_barrier_semaphore()
     for other in [left, right] + peers:
         pl.semaphore_signal(barrier, inc=1, device_id=(other,), device_id_type=MESH)
 
-    for i in range(2 * OWNED):
-        last[i] = halfs
-
-    def link(p, carry):
+    for q_ref, leg in ((qa_ref, leg_a), (qb_ref, leg_b)):
+        sign = 1.0 if leg is leg_a else -1.0
+        t = q_ref[...].astype(F32) * (2.0 / (COLS - 1)) - 1.0
+        before, now = jnp.ones_like(t), t
+        for k in range(TERMS):
+            leg[pl.ds(k * pairs, pairs), :] = before * (sign * 0.0625 * math.sqrt(2 * k + 1))
+            before, now = now, ((2 * k + 3) / (k + 2)) * t * now - ((k + 1) / (k + 2)) * before
+
+    run[halfs] = jnp.zeros(run.shape[1:], F32)
+    run_d[halfs] = jnp.zeros(run_d.shape[1:], F32)
+    run_o[halfs] = jnp.zeros(run_o.shape[1:], F32)
+    macc[...] = jnp.zeros(macc.shape, F32)
+
+    def link(p, ends):
         a = fs_ref[p] - me * OWNED
         b = ss_ref[p] - me * OWNED
         b = jnp.where(b < 0, b + n * OWNED, b)
@@ -94,49 +117,43 @@
             after = []
             for i in range(2 * OWNED):
                 hit = scene == i
-                before = jnp.where(hit, carry[i], before)
-                after.append(jnp.where(hit, h, carry[i]))
+                before = jnp.where(hit, ends[i], before)
+                after.append(jnp.where(hit, h, ends[i]))
             prev[h] = before
-            carry = tuple(after)
-        return carry
-
-    ends = lax.fori_loop(0, pairs, link, tuple(jnp.int32(halfs) for _ in range(2 * OWNED)))
+            ends = tuple(after)
+        return ends
+
+    def weights(p):
+        low = low_lanes(LANES)
+        his, los, turned, squares = [], [], [], []
+        for leg in (leg_a, leg_b):
+            hi, lo = split(leg[pl.ds(p, TERMS, stride=pairs), :])
+            his.append(hi)
+            los.append(lo)
+            wide = jnp.concatenate([hi.astype(F32), lo.astype(F32)], axis=0).T
+            turned.append(wide.astype(BF16))
+            phi = wide + swap(wide)
+            hi, lo = split(phi * phi)
+            squares.append(jnp.where(low, hi, lo))
+        wj[p] = jnp.concatenate([jnp.concatenate(his, axis=1), jnp.concatenate(los, axis=1)], axis=0)
+        wt[p] = jnp.concatenate(turned, axis=1)
+        square = jnp.concatenate(squares, axis=1)
+        w2[p] = square
+        sums = jnp.dot(jnp.ones((16, LANES), BF16), square, preferred_element_type=F32)
+        for side in range(2):
+            h = 2 * p + side
+            run_o[h] = sums[:8, side * LANES : (side + 1) * LANES] + run_o[prev[h]]
+
+    def prepare(g, ends):
+        for u in range(PREPARE):
+            ends = link(g * PREPARE + u, ends)
+        for u in range(PREPARE):
+            weights(g * PREPARE + u)
+        return ends
+
+    ends = lax.fori_loop(0, pairs // PREPARE, prepare, tuple(jnp.int32(halfs) for _ in range(2 * OWNED)))
     for i in range(2 * OWNED):
         last[i] = ends[i]
-
-    for q_ref, leg in ((qa_ref, leg_a), (qb_ref, leg_b)):
-        sign = 1.0 if leg is leg_a else -1.0
-        t = q_ref[...].astype(F32) * (2.0 / (COLS - 1)) - 1.0
-        before, now = jnp.ones_like(t), t
-        for k in range(TERMS):
-            leg[pl.ds(k * pairs, pairs), :] = before * (sign * 0.0625 * math.sqrt(2 * k + 1))
-            before, now = now, ((2 * k + 3) / (k + 2)) * t * now - ((k + 1) / (k + 2)) * before
-
-    run[halfs] = jnp.zeros(run.shape[1:], F32)
-    run_d[halfs] = jnp.zeros(run_d.shape[1:], F32)
-    run_o[halfs] = jnp.zeros(run_o.shape[1:], F32)
-    macc[...] = jnp.zeros(macc.shape, F32)
-
-    def weights(p, _):
-        tops = []
-        for side, (leg, wj, w2) in enumerate(((leg_a, wj_a, w2_a), (leg_b, wj_b, w2_b))):
-            phi = leg[pl.ds(p, TERMS, stride=pairs), :]
-            hi, lo = split(phi)
-            wj[p] = jnp.concatenate([hi, lo, hi, lo], axis=0)
-            top = jnp.concatenate([hi.astype(F32), lo.astype(F32)], axis=0)
-            tops.append(top.T.astype(BF16))
-            square = phi * phi
-            hi, lo = split(square)
-            top = jnp.concatenate([hi.astype(F32), lo.astype(F32)], axis=0)
-            turned = top.T.astype(BF16)
-            w2[p] = turned
-            sums = jnp.dot(jnp.ones((16, LANES), BF16), turned, preferred_element_type=F32)
-            h = 2 * p + side
-            run_o[h] = sums[:8] + run_o[prev[h]]
-        wt[p] = jnp.concatenate(tops, axis=1)
-        return 0
-
-    lax.fori_loop(0, pairs, weights, 0)
 
     for s in range(2 * OWNED):
         total = run_o[last[s]]
@@ -173,18 +190,23 @@
                 )
         return moves
 
+    def twice(x):
+        return jnp.concatenate([x, x], axis=0)
+
     def pull(p, size, e, la, lb):
-        weight = wt[p]
-        weight = jnp.concatenate([weight, weight], axis=0)
-        both = jnp.dot(halves(e), weight, preferred_element_type=F32)
-        gain_a = jnp.dot(halves(la * e), weight[:, :LANES], preferred_element_type=F32)
-        gain_b = jnp.dot(halves(lb * e), weight[:, LANES:], preferred_element_type=F32)
+        left_side = jnp.concatenate([halves(e), halves(la * e), halves(lb * e)], axis=0)
+        terms = jnp.dot(left_side, twice(wt[p]), preferred_element_type=F32)
+        for side in range(2):
+            lanes = slice(side * LANES, (side + 1) * LANES)
+            h = 2 * p + side
+            before = prev[h]
+            run[h, 0, :size, :] = terms[(1 + side) * size : (2 + side) * size, lanes] + run[before, 0, :size, :]
+            run[h, 1, :size, :] = terms[:size, lanes] + run[before, 1, :size, :]
+
+    def scene_total(s, size):
         low = low_lanes(size)
-        for side, gain in ((0, gain_a), (1, gain_b)):
-            offset = both[:, side * LANES : (side + 1) * LANES]
-            term = jnp.where(low, gain, offset) + swap(jnp.where(low, offset, gain))
-            h = 2 * p + side
-            run[h, :size, :] = term + run[prev[h], :size, :]
+        gain, offset = run[last[s], 0, :size, :], run[last[s], 1, :size, :]
+        return jnp.where(low, gain, offset) + swap(jnp.where(low, offset, gain))
 
     def over_pairs(body, init):
         def step(g, carry):
@@ -194,6 +216,8 @@
 
         return lax.fori_loop(0, pairs // UNROLL, step, init)
 
+    for load in loads:
+        load.wait()
     moves0 = []
     for c, (r0, size) in enumerate(chunks):
         rows = pl.ds(r0, size)
@@ -202,19 +226,21 @@
             la = ra_ref[p, rows, :].astype(F32)
             lb = rb_ref[p, rows, :].astype(F32)
             pull(p, size, lb - la, la, lb)
-            for side, (rad, w2) in enumerate(((la, w2_a), (lb, w2_b))):
-                weight = w2[p]
-                weight = jnp.concatenate([weight, weight], axis=0)
+            squares = jnp.concatenate([halves(la * la), halves(lb * lb)], axis=0)
+            terms = jnp.dot(squares, twice(w2[p]), preferred_element_type=F32)
+            for side in range(2):
                 h = 2 * p + side
-                term = jnp.dot(halves(rad * rad), weight, preferred_element_type=F32)
-                run_d[h, :size, :] = term + run_d[prev[h], :size, :]
+                run_d[h, :size, :] = (
+                    terms[side * size : (side + 1) * size, side * LANES : (side + 1) * LANES]
+                    + run_d[prev[h], :size, :]
+                )
             return carry
 
         over_pairs(start_pair, 0)
         low = low_lanes(size)
         for base, buf in ((0, own0), (OWNED, ahead0)):
             for s in range(OWNED):
-                buf[s, rows, :] = run[last[base + s], :size, :]
+                buf[s, rows, :] = scene_total(base + s, size)
             for s in range(OWNED // 2):
                 one = run_d[last[base + s], :size, :]
                 two = run_d[last[base + s + OWNED // 2], :size, :]
@@ -227,24 +253,51 @@
     def spread(s, size, z):
         low = low_lanes(size)
         turned = swap(z)
-        coef[s, 0, :size, :] = halves(jnp.where(low, z, turned))
-        coef[s, 1, :size, :] = halves(jnp.where(low, turned, z))
-
-    def apply_pair(rows, size, index):
-        def body(p, total):
+        hi, lo = split(z)
+        hi_turned, lo_turned = split(turned)
+        coef[s, 0, :size, :] = jnp.where(low, hi, lo_turned)
+        coef[s, 1, :size, :] = jnp.where(low, hi_turned, lo)
+
+    nought = jnp.zeros((LANES, LANES), BF16)
+
+    def apply_pairs(rows, size, index):
+        def product(p):
             la = ra_ref[p, rows, :].astype(F32)
             lb = rb_ref[p, rows, :].astype(F32)
-            fields = []
-            for side, wj in ((0, wj_a), (1, wj_b)):
-                both = coef[slot[2 * p + side]]
-                weight = wj[p]
-                for part in range(2):
-                    fields.append(jnp.dot(both[part, :size, :], weight, preferred_element_type=F32))
-            e = (la * fields[0] + fields[1]) + (lb * fields[2] + fields[3])
+            one, two = coef[slot[2 * p]], coef[slot[2 * p + 1]]
+            left_side = jnp.concatenate(
+                [
+                    jnp.concatenate([one[0, :size, :], one[1, :size, :]], axis=0),
+                    jnp.concatenate([two[0, :size, :], two[1, :size, :]], axis=0),
+                ],
+                axis=1,
+            )
+            left_side = jnp.concatenate([left_side, left_side], axis=1)
+            parts = []
+            for part in range(2):
+                weight = twice(wj[p, part * TERMS : (part + 1) * TERMS, :])
+                parts.append(jnp.concatenate([weight[:, :LANES], nought], axis=1))
+                parts.append(jnp.concatenate([nought, weight[:, LANES:]], axis=1))
+            fields = jnp.dot(left_side, jnp.concatenate(parts, axis=0), preferred_element_type=F32)
+            gain_a, offset_a = fields[:size, :LANES], fields[size:, :LANES]
+            gain_b, offset_b = fields[:size, LANES:], fields[size:, LANES:]
+            return (la * gain_a + lb * gain_b) + (offset_a + offset_b)
+
+        def rest(p, e, total):
+            la = ra_ref[p, rows, :].astype(F32)
+            lb = rb_ref[p, rows, :].astype(F32)
             pull(p, size, e, la, lb)
             return total + fold(e * e)
 
-        macc[index] += over_pairs(body, jnp.zeros((8, LANES), F32))
+        def step(g, total):
+            e = product(g * UNROLL)
+            for u in range(UNROLL):
+                after = product(g * UNROLL + u + 1) if u + 1 < UNROLL else None
+                total = rest(g * UNROLL + u, e, total)
+                e = after
+            return total
+
+        macc[index] += lax.fori_loop(0, pairs // UNROLL, step, jnp.zeros((8, LANES), F32))
 
     for copy in tiles:
         copy.wait()
@@ -279,10 +332,10 @@
                         macc[0] += fold(r * z)
                         macc[1] += fold(weight * (z * z))
                     spread(s, size, z)
-        apply_pair(rows, size, 1)
+        apply_pairs(rows, size, 1)
         for base, buf in ((0, own1), (OWNED, ahead1)):
             for s in range(OWNED):
-                buf[s, rows, :] = run[last[base + s], :size, :]
+                buf[s, rows, :] = scene_total(base + s, size)
         moves = transfers(c, (r0, size), (ahead1, recv_l1), (own1, recv_r1), sem_s1, sem_r1)
         for copy in moves:
             copy.start()
@@ -305,13 +358,14 @@
                     macc[2] += fold(image * w)
                     macc[3] += fold(weight * (w * w))
                 spread(s, size, w)
-        apply_pair(rows, size, 3)
+        apply_pairs(rows, size, 3)
         for base, buf in ((0, own2), (OWNED, ahead2)):
             for s in range(OWNED):
-                buf[s, rows, :] = run[last[base + s], :size, :]
+                buf[s, rows, :] = scene_total(base + s, size)
         moves = transfers(c, (r0, size), (ahead2, recv_l2), None, sem_s2, sem_r2)
-        for copy in moves:
-            copy.start()
+        if c < len(chunks) - 1:
+            for copy in moves:
+                copy.start()
         moves2.append(moves)
 
     sums = [jnp.sum(macc[i], axis=0, keepdims=True) for i in range(4)]
@@ -329,6 +383,9 @@
             )
             copies[-1].start()
             count += 1
+        if g == 0:
+            for copy in moves2[-1]:
+                copy.start()
         for j, copy in enumerate(copies):
             copy.wait()
             tile = tile + red_dst[count - len(copies) + j]
@@ -372,6 +429,7 @@
     peers = sum(size - 1 for size, _ in groups_of(n))
     smem = pl.BlockSpec(memory_space=pltpu.SMEM)
     vmem = pl.BlockSpec(memory_space=pltpu.VMEM)
+    hbm = pl.BlockSpec(memory_space=pl.ANY)
 
     def block(rows):
         return pltpu.VMEM((rows, bands, LANES), F32)
@@ -379,21 +437,21 @@
     flat = jax.ShapeDtypeStruct((bands * OWNED, LANES), F32)
     outs = pl.pallas_call(
         functools.partial(kernel, n),
-        out_shape=(flat, flat),
-        in_specs=[smem, smem, smem, vmem, vmem, vmem, vmem],
+        out_shape=(pltpu.VMEM(flat.shape, F32), pltpu.VMEM(flat.shape, F32)),
+        in_specs=[smem, smem, smem, hbm, hbm, vmem, vmem],
         out_specs=(vmem, vmem),
         scratch_shapes=[
+            pltpu.VMEM((pairs, bands, LANES), BF16),
+            pltpu.VMEM((pairs, bands, LANES), BF16),
             pltpu.VMEM((TERMS * pairs, LANES), F32),
             pltpu.VMEM((TERMS * pairs, LANES), F32),
-            pltpu.VMEM((pairs, 4 * TERMS, LANES), BF16),
-            pltpu.VMEM((pairs, 4 * TERMS, LANES), BF16),
+            pltpu.VMEM((pairs, 2 * TERMS, 2 * LANES), BF16),
             pltpu.VMEM((pairs, LANES, 2 * LANES), BF16),
-            pltpu.VMEM((pairs, LANES, LANES), BF16),
-            pltpu.VMEM((pairs, LANES, LANES), BF16),
-            pltpu.VMEM((halfs + 1, most, LANES), F32),
+            pltpu.VMEM((pairs, LANES, 2 * LANES), BF16),
+            pltpu.VMEM((halfs + 1, 2, most, LANES), F32),
             pltpu.VMEM((halfs + 1, most, LANES), F32),
             pltpu.VMEM((halfs + 1, 8, LANES), F32),
-            pltpu.VMEM((2 * OWNED, 2, most, 2 * LANES), BF16),
+            pltpu.VMEM((2 * OWNED, 2, most, LANES), BF16),
             block(12), block(12), block(12), block(12),
             block(8), block(8), block(8), block(8),
             block(8), block(8), block(8),
@@ -417,6 +475,7 @@
             pltpu.SemaphoreType.DMA((2 * len(chunks),)),
             pltpu.SemaphoreType.DMA((2 * len(chunks),)),
             pltpu.SemaphoreType.DMA((4,)),
+            pltpu.SemaphoreType.DMA((2,)),
             pltpu.SemaphoreType.DMA((peers,)),
             pltpu.SemaphoreType.DMA((peers,)),
         ],

time: 80.7 us -> 62.1 us (0.77)
  Pallas kernels: 76.2 us -> 59.4 us
  local copies, waits for them, and re-layouts: 3.17 us -> 1.85 us
    pallas_call x1, Pallas kernels: 76.2 us -> 59.4 us  [shards(): pl.pallas_call(functools.partial(kernel, n), out_shape=(pltpu.VMEM(flat.s...]
    unnamed x4 -> x2, local copies, waits for them, and re-layouts: 3.17 us -> 1.85 us
where the time goes in v1:
time: 62.1 us; the launch traced here: 61.9 us
  Pallas kernels  59.4 us (96%)
  local copies, waits for them, and re-layouts  1.85 us (3%)
  between operations  0.64 us (1%)
    pallas_call x1, Pallas kernels, shards(): pl.pallas_call(functools.partial(kernel, n), out_shape=(pltpu.VMEM(flat.s...  59.4 us
    unnamed x2, local copies, waits for them, and re-layouts  1.85 us

profile of v1, /device:TPU:1, one launch (start us, length us, event | category | flops | bytes accessed | tf_op | source)
XLA Modules:
  0.0 61.9 jit_solution(8111896907385739974)
XLA Ops:
  0.6 59.4 %shard_map.86 = (f32[1792,128]{1,0:T(8,128)S(1)}, f32[1792,128]{1,0:T(8,128)S(1)}) custom-call(s32[24]{0:T(128)} %fs_ref.1, s32[24]{0:T(128)} %ss_ref.1, f32[8]{0:T(128)} %pw_ref.1, bf16[24,224,128]{2,1,0:T(8,128)(2,1)} %ra_hbm.1, bf16[24,224,128]{2,1,0:T(8,128)(2,1)} %rb_hbm.1, s32[24,128]{1,0:T(8,128)} %qa_ref.1, s32[24,128]{1,0:T(8,128)} %qb_ref.1), custom_call_target="tpu_custom_call" | custom-call | tf_op jit(solution)/shard_map/pallas_call | solution.py:438
  60.0 0.9 %copy.11 = f32[8,28672]{1,0:T(8,128)} copy(f32[8,28672]{1,0:T(8,128)S(1)} %bitcast.11) | data formatting | bytes 1835008
  61.0 0.9 %copy.12 = f32[8,28672]{1,0:T(8,128)} copy(f32[8,28672]{1,0:T(8,128)S(1)} %bitcast.10) | data formatting | bytes 1835008

commit v2 on v1

--- a/solution.py
+++ b/solution.py
@@ -12,7 +12,7 @@
 COLS = 1024
 LANES = 128
 OWNED = 8
-UNROLL = 8
+UNROLL = 12
 PREPARE = 4
 MESH = pl.DeviceIdType.MESH
 F32 = jnp.float32
@@ -29,7 +29,7 @@
 
 
 def groups_of(n):
-    return ((8, 1), (4, 8), (4, 32)) if n == 128 else ((n, 1),)
+    return ((16, 1), (8, 16)) if n == 128 else ((n, 1),)
 
 
 def split(x):
@@ -41,6 +41,14 @@
 def halves(x):
     hi, lo = split(x)
     return jnp.concatenate([hi, lo], axis=1)
+
+
+def against(x, rows):
+    return lax.dot_general(x, rows, (((1,), (1,)), ((), ())), preferred_element_type=F32)
+
+
+def beside(x):
+    return jnp.concatenate([x, x], axis=1)
 
 
 def low_lanes(rows):
@@ -60,7 +68,7 @@
     fs_ref, ss_ref, pw_ref, ra_hbm, rb_hbm, qa_ref, qb_ref,
     out_s, out_r,
     ra_ref, rb_ref, leg_a, leg_b, wj, wt, w2,
-    run, run_d, run_o, coef,
+    run, run_d, run_o, coef, held,
     own0, ahead0, recv_l0, recv_r0,
     own1, ahead1, recv_l1, recv_r1,
     own2, ahead2, recv_l2,
@@ -124,22 +132,19 @@
         return ends
 
     def weights(p):
-        low = low_lanes(LANES)
-        his, los, turned, squares = [], [], [], []
+        his, los, rows, squares = [], [], [], []
         for leg in (leg_a, leg_b):
-            hi, lo = split(leg[pl.ds(p, TERMS, stride=pairs), :])
+            phi = leg[pl.ds(p, TERMS, stride=pairs), :]
+            hi, lo = split(phi)
             his.append(hi)
             los.append(lo)
-            wide = jnp.concatenate([hi.astype(F32), lo.astype(F32)], axis=0).T
-            turned.append(wide.astype(BF16))
-            phi = wide + swap(wide)
-            hi, lo = split(phi * phi)
-            squares.append(jnp.where(low, hi, lo))
+            rows += [hi, lo]
+            squares += list(split(phi * phi))
         wj[p] = jnp.concatenate([jnp.concatenate(his, axis=1), jnp.concatenate(los, axis=1)], axis=0)
-        wt[p] = jnp.concatenate(turned, axis=1)
-        square = jnp.concatenate(squares, axis=1)
+        wt[p] = jnp.concatenate(rows, axis=0)
+        square = jnp.concatenate(squares, axis=0)
         w2[p] = square
-        sums = jnp.dot(jnp.ones((16, LANES), BF16), square, preferred_element_type=F32)
+        sums = against(jnp.ones((16, LANES), BF16), square)
         for side in range(2):
             h = 2 * p + side
             run_o[h] = sums[:8, side * LANES : (side + 1) * LANES] + run_o[prev[h]]
@@ -195,7 +200,7 @@
 
     def pull(p, size, e, la, lb):
         left_side = jnp.concatenate([halves(e), halves(la * e), halves(lb * e)], axis=0)
-        terms = jnp.dot(left_side, twice(wt[p]), preferred_element_type=F32)
+        terms = against(left_side, beside(wt[p]))
         for side in range(2):
             lanes = slice(side * LANES, (side + 1) * LANES)
             h = 2 * p + side
@@ -227,7 +232,7 @@
             lb = rb_ref[p, rows, :].astype(F32)
             pull(p, size, lb - la, la, lb)
             squares = jnp.concatenate([halves(la * la), halves(lb * lb)], axis=0)
-            terms = jnp.dot(squares, twice(w2[p]), preferred_element_type=F32)
+            terms = against(squares, beside(w2[p]))
             for side in range(2):
                 h = 2 * p + side
                 run_d[h, :size, :] = (
@@ -260,27 +265,17 @@
 
     nought = jnp.zeros((LANES, LANES), BF16)
 
-    def apply_pairs(rows, size, index):
+    def apply_pairs(rows, size, index, between=None):
         def product(p):
             la = ra_ref[p, rows, :].astype(F32)
             lb = rb_ref[p, rows, :].astype(F32)
             one, two = coef[slot[2 * p]], coef[slot[2 * p + 1]]
-            left_side = jnp.concatenate(
-                [
-                    jnp.concatenate([one[0, :size, :], one[1, :size, :]], axis=0),
-                    jnp.concatenate([two[0, :size, :], two[1, :size, :]], axis=0),
-                ],
-                axis=1,
-            )
+            left_side = jnp.concatenate([one[0, :size, :], one[1, :size, :], two[0, :size, :], two[1, :size, :]], axis=0)
             left_side = jnp.concatenate([left_side, left_side], axis=1)
-            parts = []
-            for part in range(2):
-                weight = twice(wj[p, part * TERMS : (part + 1) * TERMS, :])
-                parts.append(jnp.concatenate([weight[:, :LANES], nought], axis=1))
-                parts.append(jnp.concatenate([nought, weight[:, LANES:]], axis=1))
-            fields = jnp.dot(left_side, jnp.concatenate(parts, axis=0), preferred_element_type=F32)
-            gain_a, offset_a = fields[:size, :LANES], fields[size:, :LANES]
-            gain_b, offset_b = fields[:size, LANES:], fields[size:, LANES:]
+            weight = jnp.concatenate([twice(wj[p, :TERMS, :]), twice(wj[p, TERMS:, :])], axis=0)
+            fields = jnp.dot(left_side, weight, preferred_element_type=F32)
+            gain_a, offset_a = fields[:size, :LANES], fields[size : 2 * size, :LANES]
+            gain_b, offset_b = fields[2 * size : 3 * size, LANES:], fields[3 * size :, LANES:]
             return (la * gain_a + lb * gain_b) + (offset_a + offset_b)
 
         def rest(p, e, total):
@@ -297,7 +292,29 @@
                 e = after
             return total
 
-        macc[index] += lax.fori_loop(0, pairs // UNROLL, step, jnp.zeros((8, LANES), F32))
+        def products(g, total):
+            for u in range(UNROLL):
+                p = g * UNROLL + u
+                e = product(p)
+                held[p, :size, :] = e
+                total = total + fold(e * e)
+            return total
+
+        def pulls(g, carry):
+            for u in range(UNROLL):
+                p = g * UNROLL + u
+                la = ra_ref[p, rows, :].astype(F32)
+                lb = rb_ref[p, rows, :].astype(F32)
+                pull(p, size, held[p, :size, :], la, lb)
+            return carry
+
+        nothing = jnp.zeros((8, LANES), F32)
+        if between is None:
+            macc[index] += lax.fori_loop(0, pairs // UNROLL, step, nothing)
+        else:
+            macc[index] += lax.fori_loop(0, pairs // UNROLL, products, nothing)
+            between()
+            lax.fori_loop(0, pairs // UNROLL, pulls, 0)
 
     for copy in tiles:
         copy.wait()
@@ -341,6 +358,25 @@
             copy.start()
         moves1.append(moves)
 
+    rounds = []
+
+    def send_sums(g, tile):
+        red_src[g] = tile
+        first_peer = sum(size - 1 for size, _ in groups[:g])
+        copies = []
+        for count in range(first_peer, first_peer + groups[g][0] - 1):
+            copy = pltpu.make_async_remote_copy(
+                red_src.at[g], red_dst.at[count], red_ssem.at[count], red_rsem.at[count],
+                device_id=(peers[count],), device_id_type=MESH,
+            )
+            copy.start()
+            copies.append((count, copy))
+        rounds.append(copies)
+
+    def start_sums():
+        sums = [jnp.sum(macc[i], axis=0, keepdims=True) for i in range(4)]
+        send_sums(0, jnp.concatenate(sums + [jnp.zeros((4, LANES), F32)], axis=0))
+
     moves2 = []
     for c, (r0, size) in enumerate(chunks):
         rows = pl.ds(r0, size)
@@ -358,37 +394,22 @@
                     macc[2] += fold(image * w)
                     macc[3] += fold(weight * (w * w))
                 spread(s, size, w)
-        apply_pairs(rows, size, 3)
+        apply_pairs(rows, size, 3, start_sums if c == len(chunks) - 1 else None)
         for base, buf in ((0, own2), (OWNED, ahead2)):
             for s in range(OWNED):
                 buf[s, rows, :] = scene_total(base + s, size)
         moves = transfers(c, (r0, size), (ahead2, recv_l2), None, sem_s2, sem_r2)
-        if c < len(chunks) - 1:
-            for copy in moves:
-                copy.start()
+        for copy in moves:
+            copy.start()
         moves2.append(moves)
 
-    sums = [jnp.sum(macc[i], axis=0, keepdims=True) for i in range(4)]
-    tile = jnp.concatenate(sums + [jnp.zeros((4, LANES), F32)], axis=0)
-    count = 0
-    for g, (size, stride) in enumerate(groups):
-        red_src[g] = tile
-        copies = []
-        for j in range(1, size):
-            copies.append(
-                pltpu.make_async_remote_copy(
-                    red_src.at[g], red_dst.at[count], red_ssem.at[count], red_rsem.at[count],
-                    device_id=(peers[count],), device_id_type=MESH,
-                )
-            )
-            copies[-1].start()
-            count += 1
-        if g == 0:
-            for copy in moves2[-1]:
-                copy.start()
-        for j, copy in enumerate(copies):
+    for g in range(len(groups)):
+        if g > 0:
+            send_sums(g, tile)
+        tile = red_src[g]
+        for count, copy in rounds[g]:
             copy.wait()
-            tile = tile + red_dst[count - len(copies) + j]
+            tile = tile + red_dst[count]
     tile = jnp.sum(tile, axis=1, keepdims=True)
     m0, m1, m2, m3 = (tile[i : i + 1, :] for i in range(4))
     first = m0 / m1
@@ -446,12 +467,13 @@
             pltpu.VMEM((TERMS * pairs, LANES), F32),
             pltpu.VMEM((TERMS * pairs, LANES), F32),
             pltpu.VMEM((pairs, 2 * TERMS, 2 * LANES), BF16),
-            pltpu.VMEM((pairs, LANES, 2 * LANES), BF16),
-            pltpu.VMEM((pairs, LANES, 2 * LANES), BF16),
+            pltpu.VMEM((pairs, 4 * TERMS, LANES), BF16),
+            pltpu.VMEM((pairs, 4 * TERMS, LANES), BF16),
             pltpu.VMEM((halfs + 1, 2, most, LANES), F32),
             pltpu.VMEM((halfs + 1, most, LANES), F32),
             pltpu.VMEM((halfs + 1, 8, LANES), F32),
             pltpu.VMEM((2 * OWNED, 2, most, LANES), BF16),
+            pltpu.VMEM((pairs, most, LANES), F32),
             block(12), block(12), block(12), block(12),
             block(8), block(8), block(8), block(8),
             block(8), block(8), block(8),

time: 62.1 us -> 58.5 us (0.942)
  Pallas kernels: 59.4 us -> 56 us
    pallas_call x1, Pallas kernels: 59.4 us -> 56 us  [shards(): pl.pallas_call(functools.partial(kernel, n), out_shape=(pltpu.VMEM(flat.s...]
where the time goes in v2:
time: 58.5 us
  Pallas kernels  56 us (96%)
  local copies, waits for them, and re-layouts  1.85 us (3%)
  between operations  0.64 us (1%)
    pallas_call x1, Pallas kernels, shards(): pl.pallas_call(functools.partial(kernel, n), out_shape=(pltpu.VMEM(flat.s...  56 us
    unnamed x2, local copies, waits for them, and re-layouts  1.85 us

profile of v2, /device:TPU:1, one launch (start us, length us, event | category | flops | bytes accessed | tf_op | source)
XLA Modules:
  0.0 58.5 jit_solution(3566985808682711755)
XLA Ops:
  0.6 56.0 %shard_map.86 = (f32[1792,128]{1,0:T(8,128)S(1)}, f32[1792,128]{1,0:T(8,128)S(1)}) custom-call(s32[24]{0:T(128)} %fs_ref.1, s32[24]{0:T(128)} %ss_ref.1, f32[8]{0:T(128)} %pw_ref.1, bf16[24,224,128]{2,1,0:T(8,128)(2,1)} %ra_hbm.1, bf16[24,224,128]{2,1,0:T(8,128)(2,1)} %rb_hbm.1, s32[24,128]{1,0:T(8,128)} %qa_ref.1, s32[24,128]{1,0:T(8,128)} %qb_ref.1), custom_call_target="tpu_custom_call" | custom-call | tf_op jit(solution)/shard_map/pallas_call | solution.py:459
  56.6 0.9 %copy.11 = f32[8,28672]{1,0:T(8,128)} copy(f32[8,28672]{1,0:T(8,128)S(1)} %bitcast.11) | data formatting | bytes 1835008
  57.6 0.9 %copy.12 = f32[8,28672]{1,0:T(8,128)} copy(f32[8,28672]{1,0:T(8,128)S(1)} %bitcast.10) | data formatting | bytes 1835008

commit v3 on v2

--- a/solution.py
+++ b/solution.py
@@ -327,7 +327,7 @@
     for c, (r0, size) in enumerate(chunks):
         rows = pl.ds(r0, size)
         for copy in moves0[c]:
-            copy.wait()
+            copy.wait_recv()
         low = low_lanes(size)
         for base, mine, theirs in ((0, own0, recv_l0), (OWNED, ahead0, recv_r0)):
             for half in range(2):
@@ -381,7 +381,7 @@
     for c, (r0, size) in enumerate(chunks):
         rows = pl.ds(r0, size)
         for copy in moves1[c]:
-            copy.wait()
+            copy.wait_recv()
         for base, mine, theirs in ((0, own1, recv_l1), (OWNED, ahead1, recv_r1)):
             for row in range(OWNED):
                 s = base + row
@@ -421,7 +421,7 @@
 
     for c, (r0, size) in enumerate(chunks):
         for copy in moves2[c]:
-            copy.wait()
+            copy.wait_recv()
         half = size // 2
         low = low_lanes(half)
         for s in range(OWNED):
@@ -440,6 +440,10 @@
             for out, even, odd in ((out_s, parts[0][0], parts[1][0]), (out_r, parts[0][1], parts[1][1])):
                 out[pl.ds((r0 // 2) * OWNED + s, half, stride=OWNED), :] = jnp.where(low, even, swap(odd))
                 out[pl.ds((bands // 2 + r0 // 2) * OWNED + s, half, stride=OWNED), :] = jnp.where(low, swap(even), odd)
+
+    for moves in moves0 + moves1 + moves2:
+        for copy in moves:
+            copy.wait_send()
 
 
 def shards(n, first_scene, second_scene, rad_first, rad_second, pos_first, pos_second, prior_weight):

time: 58.5 us -> 58.5 us (level)
  no operation moved by 1% of the time
where the time goes in v3:
time: 58.5 us; the launch traced here: 58.3 us
  Pallas kernels  55.8 us (95%)
  local copies, waits for them, and re-layouts  1.85 us (3%)
  between operations  0.64 us (1%)
    pallas_call x1, Pallas kernels, shards(): pl.pallas_call(functools.partial(kernel, n), out_shape=(pltpu.VMEM(flat.s...  55.8 us
    unnamed x2, local copies, waits for them, and re-layouts  1.85 us

profile of v3, /device:TPU:1, one launch (start us, length us, event | category | flops | bytes accessed | tf_op | source)
XLA Modules:
  0.0 58.3 jit_solution(9381094032409559573)
XLA Ops:
  0.6 55.8 %shard_map.86 = (f32[1792,128]{1,0:T(8,128)S(1)}, f32[1792,128]{1,0:T(8,128)S(1)}) custom-call(s32[24]{0:T(128)} %fs_ref.1, s32[24]{0:T(128)} %ss_ref.1, f32[8]{0:T(128)} %pw_ref.1, bf16[24,224,128]{2,1,0:T(8,128)(2,1)} %ra_hbm.1, bf16[24,224,128]{2,1,0:T(8,128)(2,1)} %rb_hbm.1, s32[24,128]{1,0:T(8,128)} %qa_ref.1, s32[24,128]{1,0:T(8,128)} %qb_ref.1), custom_call_target="tpu_custom_call" | custom-call | tf_op jit(solution)/shard_map/pallas_call | solution.py:463
  56.4 0.9 %copy.11 = f32[8,28672]{1,0:T(8,128)} copy(f32[8,28672]{1,0:T(8,128)S(1)} %bitcast.11) | data formatting | bytes 1835008
  57.3 0.9 %copy.12 = f32[8,28672]{1,0:T(8,128)} copy(f32[8,28672]{1,0:T(8,128)S(1)} %bitcast.10) | data formatting | bytes 1835008
